TPU v7x, 256 devices: a whole 4x4x8 slice. The times are simulated.
256 devices in a mesh: seg: 4 (over z_hi, core), space: 64 (over y, x, z_lo).
Axes of the slice: x: 4, y: 4, z: 8 (z_hi: 2, z_lo: 4; z = z_hi * 4 + z_lo), core: 2. Of those that a mesh axis runs over, the one named last changes fastest.
Arguments:
- directions: float32 [4, 16, 256, 64, 128], P('seg', None, 'space'), may hold values from -100 to 100
- adjoint: float32 [4, 256, 64, 128], P('seg', 'space'), may hold values from -1000 to 1000
- velocity: float32 [4, 3, 256, 64, 128], P('seg', None, 'space'), may hold values from -1 to 1
- diffusivity: float32 [4, 256, 64, 128], P('seg', 'space'), may hold values from 0.05 to 0.15
- objective_source: float32 [4, 256, 64, 128], P('seg', 'space'), may hold values from -6 to 6
- segment_start: int32 [4], P('seg'), may hold values from 0 to 999
Outputs:
- basis_rows: float32 [4, 16, 256, 64, 128], P('seg', None, 'space')
- factor_upper: float32 [4, 16, 16], P('seg')
- coefficients: float32 [4, 16], P('seg')
- shadow: float32 [4, 256, 64, 128], P('seg', 'space')
- gradient: float32 [256, 64, 128], P('space', 'seg')
All inputs are finite; a program needn't handle non-finite values.
Results may differ from a plain program's by a relative error of at most 0.0003.
Values sent between devices are 32-bit elements; how exact they have to be, the bound alone decides.
A program may use at most 64 MiB of HBM per device.

v0:
```python
import math

import jax
import jax.numpy as jnp
from jax import lax
from jax.sharding import PartitionSpec as P


def with_halo(array, sides, width):
    for axis, dim in sides:
        size, length = (lax.axis_size(axis), array.shape[dim])
        up = [(i, (i + 1) % size) for i in range(size)]
        down = [(j, i) for i, j in up]
        last = lax.slice_in_dim(array, length - width, length, axis=dim)
        first = lax.slice_in_dim(array, 0, width, axis=dim)
        before = lax.ppermute(last, axis, up)
        after = lax.ppermute(first, axis, down)
        array = jnp.concatenate([before, array, after], axis=dim)
    return array


def modulation(window_start, section):
    phase_step = (window_start + 2 - section) % 64
    return 1.0 + 0.5 * jnp.sin(2.0 * math.pi * phase_step.astype(jnp.float32) / 64.0)


def advance(extended, diffusivity, velocity, strength):
    middle = extended[:, 1:-1]
    forward_x = extended[:, 2:]
    behind_x = extended[:, :-2]
    wall_zero = jnp.zeros_like(middle[:, :, :1])
    forward_y = jnp.concatenate([middle[:, :, 1:], wall_zero], axis=2)
    behind_y = jnp.concatenate([wall_zero, middle[:, :, :-1]], axis=2)
    forward_z = jnp.roll(middle, -1, axis=3)
    behind_z = jnp.roll(middle, 1, axis=3)
    laplace = forward_x + behind_x + forward_y + behind_y + forward_z + behind_z - 6.0 * middle
    transport = (
        velocity[0] * (forward_x - behind_x)
        + velocity[1] * (forward_y - behind_y)
        + velocity[2] * (forward_z - behind_z)
    )
    return middle + diffusivity * laplace + 0.5 * strength * transport


def body(directions, adjoint, velocity, diffusivity, objective_source, segment_start):
    count_dirs = directions.shape[1]
    stacked = jnp.concatenate([directions[0], adjoint[0][None]], axis=0)
    flow = velocity[0]
    spread = diffusivity[0]
    source = objective_source[0]
    window_start = segment_start[0]
    first_adjoint = source
    for section in (1, 2):
        extended = with_halo(stacked, (("space", 1),), 1)
        stacked = advance(extended, spread, flow, modulation(window_start, section))
        stacked = stacked.at[-1].add(source)
        if section == 1:
            first_adjoint = stacked[-1]
    flattened = stacked.reshape(count_dirs + 1, -1)
    cell_count = flattened.shape[1] * lax.axis_size("space")
    partial_sums = jnp.dot(
        flattened[:count_dirs], flattened[:count_dirs].T, precision=lax.Precision.HIGHEST
    )
    summed = lax.psum(partial_sums, "space") / cell_count
    triangle = jnp.linalg.cholesky(summed)
    inverse = jax.scipy.linalg.solve_triangular(
        triangle, jnp.eye(count_dirs, dtype=triangle.dtype), lower=True
    )
    basis_rows = jnp.dot(inverse, flattened[:count_dirs], precision=lax.Precision.HIGHEST)
    local_along = jnp.dot(basis_rows, flattened[count_dirs], precision=lax.Precision.HIGHEST)
    coefficients = lax.psum(local_along, "space") / cell_count
    shadow = flattened[count_dirs] - jnp.dot(
        coefficients, basis_rows, precision=lax.Precision.HIGHEST
    )
    shadow = shadow.reshape(source.shape)
    gradient = lax.psum_scatter(first_adjoint + shadow, "seg", scatter_dimension=1, tiled=True)
    basis_out = basis_rows.reshape((1,) + directions.shape[1:])
    return (basis_out, triangle.T[None], coefficients[None], shadow[None], gradient)


def solution(mesh):
    return jax.shard_map(
        body,
        mesh=mesh,
        in_specs=(
            P("seg", None, "space", None, None),
            P("seg", "space", None, None),
            P("seg", None, "space", None, None),
            P("seg", "space", None, None),
            P("seg", "space", None, None),
            P("seg"),
        ),
        out_specs=(
            P("seg", None, "space", None, None),
            P("seg", None, None),
            P("seg", None),
            P("seg", "space", None, None),
            P("space", "seg", None),
        ),
        check_vma=False,
    )
```

profile of v0, /device:TPU:1, one launch (start us, length us, event | category | flops | bytes accessed | tf_op | source)
XLA Modules:
  0.0 514.4 jit_solution(889202790034715220)
XLA Ops:
  7.2 2.8 copy.51
  10.3 9.9 %collective-permute-start = (f32[17,1,64,128]{3,2,1,0:T(8,128)S(1)}, f32[17,1,64,128]{3,2,1,0:T(8,128)}, u32[]{:S(2)}, u32[]{:S(2)}) collective-permute-start(f32[17,1,64,128]{3,2,1,0:T(8,128)S(1)} %copy.28), channel_id=1, source_target_pairs={{1,0},{2,1},{3,2},{4,3},{5,4},{6,5},{7,6},{8,7},{9,8},{10,9},{11,1... | collective-permute-start | bytes 1671176 | tf_op jit(solution)/shard_map/ppermute | solution.py:17
  21.1 3.0 fusion.4
  27.7 3.9 collective-permute-done
  31.6 1.4 copy.29
  33.0 11.5 %collective-permute-done.1 = f32[17,1,64,128]{3,2,1,0:T(8,128)} collective-permute-done((f32[17,1,64,128]{3,2,1,0:T(8,128)}, f32[17,1,64,128]{3,2,1,0:T(8,128)}, u32[]{:S(2)}, u32[]{:S(2)}) %collective-permute-start.1) | collective-permute-done | bytes 557088 | tf_op jit(solution)/shard_map/ppermute | solution.py:16
  44.5 1.4 copy.31
  45.9 5.5 %multiply_add_fusion.1 = f32[17,4,64,128]{3,0,2,1:T(8,128)S(1)} fusion(f32[1,4,64,128]{3,0,2,1:T(1,128)S(1)} %bitcast.70, f32[16,4,64,128]{3,0,2,1:T(8,128)S(1)} %bitcast.63, f32[17,4,64,127]{3,0,2,1:T(8,128)S(1)} %get-tuple-element.57, f32[17,4,64,1]{3,0,2,1:T(8,128)S(1)} %get-tuple-element.59, f32[17,4,64,1]{3,0,2,1:T(8,128)S(1)} %get-tuple-element.58, ...), kind=kLoop, calls=%fused_computation.32 | loop fusion | flops 14483456 | bytes 14938116 | tf_op jit(solution)/shard_map/add | solution.py:42
  51.6 2.6 scatter-add.4
  55.6 3.0 collective-permute-start.2
  58.6 2.0 fusion.22
  61.6 18.7 %collective-permute-done.2 = f32[17,1,64,128]{3,2,1,0:T(8,128)S(1)} collective-permute-done((f32[17,1,64,128]{3,2,1,0:T(8,128)S(1)}, f32[17,1,64,128]{3,2,1,0:T(8,128)S(1)}, u32[]{:S(2)}, u32[]{:S(2)}) %collective-permute-start.2) | collective-permute-done | bytes 557088 | tf_op jit(solution)/shard_map/ppermute | solution.py:17
  80.4 1.2 copy.34
  82.1 1.2 copy.36
  83.4 5.9 %multiply_add_fusion = f32[17,4,64,128]{3,0,2,1:T(8,128)S(1)} fusion(f32[17,4,64,128]{3,0,2,1:T(8,128)S(1)} %scatter-add.4, f32[17,4,64,127]{3,0,2,1:T(8,128)S(1)} %get-tuple-element.49, f32[17,4,64,1]{3,0,2,1:T(8,128)S(1)} %get-tuple-element.51, f32[17,4,64,1]{3,0,2,1:T(8,128)S(1)} %get-tuple-element.50, f32[17,4,64,127]{3,0,2,1:T(8,128)S(1)} %get-tuple-element.48, ...), kind=kLoop, calls=%fused_computation.31 | loop fusion | flops 12812288 | bytes 14938116 | tf_op jit(solution)/shard_map/add | solution.py:42
  89.2 2.9 convolution_bitcast_fusion
  93.4 158.8 %psum.14 = f32[16,16]{0,1:T(8,128)S(1)} all-reduce(f32[16,16]{0,1:T(8,128)S(1)} %convolution_bitcast_fusion), channel_id=1, replica_groups=mesh['seg'=4,'space'=64] {'space'}, use_global_device_ids=true, to_apply=%region_0.1 | all-reduce | flops 256 | bytes 2048 | tf_op jit(solution)/shard_map/psum | solution.py:64
  252.3 1.5 cholesky.17
  255.1 1.2 custom-call.7
  257.2 2.8 fusion.6
  260.1 2.6 convolution_bitcast_fusion.1
  262.7 154.2 %psum.15 = f32[16]{0:T(128)S(1)} all-reduce(f32[16]{0:T(128)S(1)} %convolution_bitcast_fusion.1), channel_id=1, replica_groups=mesh['seg'=4,'space'=64] {'space'}, use_global_device_ids=true, to_apply=%region_3.4 | all-reduce | flops 16 | bytes 128 | tf_op jit(solution)/shard_map/psum | solution.py:71
  419.4 1.7 copy.45
  421.7 85.9 %reduce-scatter.2.cloned.1.call-done = f32[4,16,128]{2,1,0:T(8,128)} async-done(((f32[4,64,128]{2,1,0:T(8,128)}), f32[4,16,128]{2,1,0:T(8,128)}) %reduce-scatter.2.cloned.1.call-update) | async-done | bytes 32784 | tf_op jit(solution)/shard_map/reduce_scatter | solution.py:76
  (58 shorter events, 13.5 us)
Async XLA Ops:
  7.2 2.9 copy-start.3
  7.2 500.4 %reduce-scatter.2.cloned.1.call-start = ((), (), s32[]{:S(2)}) async-start(), calls=%async_computation.1 | async-start | bytes 163840 | tf_op jit(solution)/shard_map/reduce_scatter | solution.py:76
  10.1 16.6 %copy-start = (f32[1,16,4,64,128]{4,1,3,2,0:T(8,128)}, f32[1,16,4,64,128]{4,1,3,2,0:T(8,128)S(1)}, u32[]{:S(2)}) copy-start(f32[1,16,4,64,128]{4,1,3,2,0:T(8,128)S(1)} %copy.51) | copy-start | bytes 6291460
  10.3 21.3 %collective-permute-start = (f32[17,1,64,128]{3,2,1,0:T(8,128)S(1)}, f32[17,1,64,128]{3,2,1,0:T(8,128)}, u32[]{:S(2)}, u32[]{:S(2)}) collective-permute-start(f32[17,1,64,128]{3,2,1,0:T(8,128)S(1)} %copy.28), channel_id=1, source_target_pairs={{1,0},{2,1},{3,2},{4,3},{5,4},{6,5},{7,6},{8,7},{9,8},{10,9},{11,1... | collective-permute-start | bytes 1671176 | tf_op jit(solution)/shard_map/ppermute | solution.py:17
  21.1 3.0 copy-start.12
  21.1 23.4 %collective-permute-start.1 = (f32[17,1,64,128]{3,2,1,0:T(8,128)}, f32[17,1,64,128]{3,2,1,0:T(8,128)}, u32[]{:S(2)}, u32[]{:S(2)}) collective-permute-start(f32[17,1,64,128]{3,2,1,0:T(8,128)} %copy.30), channel_id=1, source_target_pairs={{0,1},{1,2},{2,3},{3,4},{4,5},{5,6},{6,7},{7,8},{8,9},{9,10},{10,1... | collective-permute-start | bytes 1671176 | tf_op jit(solution)/shard_map/ppermute | solution.py:16
  26.6 19.3 %copy-start.2 = (f32[17,4,63,128]{3,0,2,1:T(8,128)S(1)}, f32[17,4,63,128]{3,0,2,1:T(8,128)}, u32[]{:S(2)}) copy-start(f32[17,4,63,128]{3,0,2,1:T(8,128)} %get-tuple-element.54) | copy-start | bytes 6580228
  26.6 19.3 %copy-start.4 = (f32[4,64,128]{2,1,0:T(8,128)S(1)}, f32[4,64,128]{2,1,0:T(8,128)}, u32[]{:S(2)}) copy-start(f32[4,64,128]{2,1,0:T(8,128)} %get-tuple-element.62) | copy-start | bytes 393220
  26.6 19.3 %copy-start.8 = (f32[1,4,64,128]{3,2,1,0:T(8,128)S(1)}, f32[1,4,64,128]{3,2,1,0:T(8,128)}, u32[]{:S(2)}) copy-start(f32[1,4,64,128]{3,2,1,0:T(8,128)} %param.13) | copy-start | bytes 393220
  27.7 18.2 %copy-start.1 = (f32[1,16,4,64,128]{4,1,3,2,0:T(8,128)S(1)}, f32[1,16,4,64,128]{4,1,3,2,0:T(8,128)}, u32[]{:S(2)}) copy-start(f32[1,16,4,64,128]{4,1,3,2,0:T(8,128)} %copy-done) | copy-start | bytes 6291460
  45.9 5.6 %copy-start.10 = (f32[1,4,64,128]{3,2,1,0:T(8,128)S(1)}, f32[1,4,64,128]{3,2,1,0:T(8,128)}, u32[]{:S(2)}) copy-start(f32[1,4,64,128]{3,2,1,0:T(8,128)} %param.14) | copy-start | bytes 393220
  51.6 3.7 copy-start.6
  55.6 24.8 %collective-permute-start.2 = (f32[17,1,64,128]{3,2,1,0:T(8,128)S(1)}, f32[17,1,64,128]{3,2,1,0:T(8,128)S(1)}, u32[]{:S(2)}, u32[]{:S(2)}) collective-permute-start(f32[17,1,64,128]{3,2,1,0:T(8,128)S(1)} %copy.33), channel_id=1, source_target_pairs={{1,0},{2,1},{3,2},{4,3},{5,4},{6,5},{7,6},{8,7},{9,8},{10,9},{11,1... | collective-permute-start | bytes 1671176 | tf_op jit(solution)/shard_map/ppermute | solution.py:17
  58.6 23.5 %collective-permute-start.3 = (f32[17,1,64,128]{3,2,1,0:T(8,128)S(1)}, f32[17,1,64,128]{3,2,1,0:T(8,128)S(1)}, u32[]{:S(2)}, u32[]{:S(2)}) collective-permute-start(f32[17,1,64,128]{3,2,1,0:T(8,128)S(1)} %copy.35), channel_id=1, source_target_pairs={{0,1},{1,2},{2,3},{3,4},{4,5},{5,6},{6,7},{7,8},{8,9},{9,10},{10,1... | collective-permute-start | bytes 1671176 | tf_op jit(solution)/shard_map/ppermute | solution.py:16
  60.6 22.8 %copy-start.5 = (f32[4,64,128]{2,1,0:T(8,128)S(1)}, f32[4,64,128]{2,1,0:T(8,128)}, u32[]{:S(2)}) copy-start(f32[4,64,128]{2,1,0:T(8,128)} %get-tuple-element.62) | copy-start | bytes 393220
  60.6 22.8 %copy-start.9 = (f32[1,4,64,128]{3,2,1,0:T(8,128)S(1)}, f32[1,4,64,128]{3,2,1,0:T(8,128)}, u32[]{:S(2)}) copy-start(f32[1,4,64,128]{3,2,1,0:T(8,128)} %param.13) | copy-start | bytes 393220
  260.1 158.0 %copy-start.7 = (f32[1,4,64,128]{3,0,2,1:T(1,128)S(1)}, f32[1,4,64,128]{3,0,2,1:T(1,128)}, u32[]{:S(2)}) copy-start(f32[1,4,64,128]{3,0,2,1:T(1,128)} %copy-done.6) | copy-start | bytes 393220
  418.0 89.5 %copy-start.11 = (f32[32768]{0:T(1024)}, f32[32768]{0:T(1024)S(1)}, u32[]{:S(2)}) copy-start(f32[32768]{0:T(1024)S(1)} %sub.40) | copy-start | bytes 393220
Sparse Core Ops, SparseCore 0:
  418.9 88.6 reduce-scatter.1
where the time goes:
time: 515 us; the launch traced here: 514 us
  blocking collectives  313 us (61%)
  waiting for transfers between devices  121 us (23%)
  other arithmetic  22.9 us (4%)
  local copies, waits for them, and re-layouts  20.1 us (4%)
  between operations  15.2 us (3%)
  starting transfers between devices  13 us (3%)
  matrix products  9.58 us (2%)
    psum x1, blocking collectives, body(): summed = lax.psum(partial_sums, 'space') / cell_count  159 us
    psum x1, blocking collectives, body(): coefficients = lax.psum(local_along, 'space') / cell_count  154 us
    reduce_scatter x1, waiting for transfers between devices, body(): lax.psum_scatter(first_adjoint + shadow, 'seg', scatter_dimension=1, tile...  85.9 us
    ppermute x2, waiting for transfers between devices, with_halo(): after = lax.ppermute(first, axis, down)  22.6 us
    ppermute x2, starting transfers between devices, with_halo(): after = lax.ppermute(first, axis, down)  12.9 us
    ppermute x2, waiting for transfers between devices, with_halo(): before = lax.ppermute(last, axis, up)  12 us
    add x2, other arithmetic, advance(): return middle + diffusivity * laplace + 0.5 * strength * transport  11.4 us
  transfers between devices with their start and end apart: 5, of which 5 were waited for; matrix products, arithmetic and copies ran while one was open for 3% of the time, Pallas kernels for 0%

commit v1 on v0

v1 whole, which is shorter than its diff:
```python
import functools
import math

import jax
import jax.numpy as jnp
from jax import lax
from jax.experimental import pallas as pl
from jax.experimental.pallas import tpu as pltpu
from jax.sharding import PartitionSpec as P

MESH = pl.DeviceIdType.MESH
DIRS = 16
FIELDS = 17
LAYERS = 4
BLOCKS = 8
POS = LAYERS * BLOCKS
AHEAD = 4
F32 = jnp.float32


def place_of(size):
    depth = min(4, size)
    width = min(4, size // depth)
    height = size // (depth * width)
    return height, width, depth


def peers_of(me, size):
    height, width, depth = place_of(size)
    z = lax.rem(me, depth)
    x = lax.rem(lax.div(me, depth), width)
    y = lax.div(me, depth * width)
    stages = [
        [(y * width + lax.rem(x + d, width)) * depth + z for d in range(1, width)],
        [(lax.rem(y + d, height) * width + x) * depth + z for d in range(1, height)],
        [(y * width + x) * depth + lax.rem(z + d, depth) for d in range(1, depth)],
    ]
    return [stage for stage in stages if stage]


def layer(ref, lead, x):
    return ref[(*lead, pl.ds(BLOCKS * x, BLOCKS))].reshape(BLOCKS * 8, 128)


def stencil(here, ahead, behind, coef, step, x):
    c = [layer(coef, (step, n), x) for n in range(7)]
    out = c[0] * here + c[1] * ahead + c[2] * behind
    out = out + c[3] * pltpu.roll(here, BLOCKS * 8 - 1, 0) + c[4] * pltpu.roll(here, 1, 0)
    return out + c[5] * pltpu.roll(here, 127, 1) + c[6] * pltpu.roll(here, 1, 1)


def kernel(
    size, segs, cells,
    start_ref, dirs_ref, adj_ref, vel_ref, dif_ref, src_ref,
    basis_ref, upper_ref, coef_ref, shadow_ref, grad_ref,
    f_all, g_all, w_all, f_halo, g_halo, coef, vel, dif, src, basis,
    gram, gram_cur, gram_got, along_cur, along_got, columns, inverse_rows, spread, inverse, weights, terms, arrived,
    load_sem, store_sem, f_send, f_recv, g_send, g_recv,
    gram_send, gram_recv, along_send, along_recv, term_send, term_recv,
):
    seg = lax.axis_index("seg")
    me = lax.axis_index("space")
    right, left = lax.rem(me + 1, size), lax.rem(me + size - 1, size)
    stages = peers_of(me, size)

    loads = [
        pltpu.make_async_copy(dirs_ref, f_all.at[pl.ds(0, DIRS)], load_sem.at[0]),
        pltpu.make_async_copy(adj_ref, f_all.at[DIRS], load_sem.at[1]),
        pltpu.make_async_copy(vel_ref, vel, load_sem.at[2]),
        pltpu.make_async_copy(dif_ref, dif, load_sem.at[3]),
        pltpu.make_async_copy(src_ref, src, load_sem.at[4]),
    ]
    for load in loads:
        load.start()

    barrier = pltpu.get_barrier_semaphore()
    greeted = [{"space": left}, {"space": right}]
    greeted += [{"space": peer} for stage in stages for peer in stage]
    greeted += [{"seg": lax.rem(seg + d, segs)} for d in range(1, segs)]
    for device in greeted:
        pl.semaphore_signal(barrier, inc=1, device_id=device, device_id_type=MESH)

    def clear(n, _):
        w_all[n] = jnp.zeros((POS, 8, 128), F32)
        return 0

    lax.fori_loop(0, FIELDS, clear, 0)
    gram[...] = jnp.zeros_like(gram)
    for load in loads:
        load.wait()
    pl.semaphore_wait(barrier, len(greeted))

    def halo(source, landing, send, recv, n, side):
        edge = BLOCKS * (LAYERS - 1) if side == 0 else 0
        return pltpu.make_async_remote_copy(
            source.at[n, pl.ds(edge, BLOCKS)],
            landing.at[side, n],
            send.at[side, n],
            recv.at[side, n],
            device_id={"space": right if side == 0 else left},
            device_id_type=MESH,
        )

    f_copy = functools.partial(halo, f_all, f_halo, f_send, f_recv)
    g_copy = functools.partial(halo, g_all, g_halo, g_send, g_recv)
    for n in range(AHEAD):
        for side in range(2):
            f_copy(n, side).start()

    row = lax.broadcasted_iota(jnp.int32, (BLOCKS * 8, 128), 0)
    for step in range(2):
        phase = jnp.full((8, 128), start_ref[0], jnp.int32) + (1 - step)
        turn = lax.rem(phase, jnp.full((8, 128), 64, jnp.int32)).astype(F32)
        half = 0.5 * (1.0 + 0.5 * jnp.sin(2.0 * math.pi * turn / 64.0))
        half = jnp.broadcast_to(half[0:1], (BLOCKS * 8, 128))

        def prepare(x, _, step=step, half=half):
            spot = pl.ds(BLOCKS * x, BLOCKS)
            d = layer(dif, (), x)
            values = [1.0 - 6.0 * d]
            for axis in range(3):
                drift = half * layer(vel, (axis,), x)
                values += [d + drift, d - drift]
            values[3] = jnp.where(row == BLOCKS * 8 - 1, 0.0, values[3])
            values[4] = jnp.where(row == 0, 0.0, values[4])
            for n in range(7):
                coef[step, n, spot] = values[n].reshape(BLOCKS, 8, 128)
            return 0

        lax.fori_loop(0, LAYERS, prepare, 0)

    def advance(step, source, landing, target, n, layers):
        for x in layers:
            here = layer(source, (n,), x)
            ahead = layer(source, (n,), x + 1) if x < LAYERS - 1 else landing[1, n].reshape(BLOCKS * 8, 128)
            behind = layer(source, (n,), x - 1) if x > 0 else landing[0, n].reshape(BLOCKS * 8, 128)
            out = stencil(here, ahead, behind, coef, step, x)
            target[n, pl.ds(BLOCKS * x, BLOCKS)] = out.reshape(BLOCKS, 8, 128)

        @pl.when(n == DIRS)
        def _():
            for x in layers:
                spot = pl.ds(BLOCKS * x, BLOCKS)
                target[n, spot] = target[n, spot] + src[spot]

    def first(n, _):
        for side in range(2):
            f_copy(n, side).wait_recv()
        advance(0, f_all, f_halo, g_all, n, (0, 3))
        for side in range(2):
            f_copy(n, side).wait_send()

        @pl.when(n + AHEAD < FIELDS)
        def _():
            for side in range(2):
                f_copy(n + AHEAD, side).start()

        @pl.when(n + AHEAD >= FIELDS)
        def _():
            for side in range(2):
                g_copy(n + AHEAD - FIELDS, side).start()

        advance(0, f_all, f_halo, g_all, n, (1, 2))
        return 0

    lax.fori_loop(0, FIELDS, first, 0)

    lane = lax.broadcasted_iota(jnp.int32, (DIRS, 128), 1)

    def products(n):
        def at(p, total):
            return total + w_all[0:DIRS, p] * w_all[n, p][None]

        total = lax.fori_loop(0, POS, at, jnp.zeros((DIRS, 8, 128), F32), unroll=4)
        return jnp.sum(jnp.sum(total, axis=1), axis=1, keepdims=True)

    def second(n):
        advance(1, g_all, g_halo, w_all, n, (1, 2))
        for side in range(2):
            g_copy(n, side).wait_recv()
            g_copy(n, side).wait_send()

        @pl.when(n + AHEAD < FIELDS)
        def _():
            for side in range(2):
                g_copy(n + AHEAD, side).start()

        advance(1, g_all, g_halo, w_all, n, (0, 3))
        return products(n)

    def gram_row(n, _):
        gram[...] = jnp.where(lane == n, second(n), gram[...])
        return 0

    lax.fori_loop(0, DIRS, gram_row, 0)

    def exchange(cur, got, send, recv, k):
        base = sum(len(stage) for stage in stages[:k])
        return [
            pltpu.make_async_remote_copy(
                cur.at[k], got.at[base + n], send.at[base + n], recv.at[base + n],
                device_id={"space": peer}, device_id_type=MESH,
            )
            for n, peer in enumerate(stages[k])
        ]

    gram_parts = functools.partial(exchange, gram_cur, gram_got, gram_send, gram_recv)
    along_parts = functools.partial(exchange, along_cur, along_got, along_send, along_recv)

    def collect(parts, cur, got, k):
        base = sum(len(stage) for stage in stages[:k])
        for copy in parts(k):
            copy.wait_recv()
        total = cur[k]
        for n in range(len(stages[k])):
            total = total + got[base + n]
        cur[k + 1] = total

    gram_cur[0] = gram[...]
    for copy in gram_parts(0):
        copy.start()
    along_cur[0] = jnp.broadcast_to(second(DIRS), (DIRS, 128))
    for copy in along_parts(0):
        copy.start()
    count = len(stages)
    for k in range(count):
        collect(gram_parts, gram_cur, gram_got, k)
        if k + 1 < count:
            for copy in gram_parts(k + 1):
                copy.start()
            collect(along_parts, along_cur, along_got, k)
            for copy in along_parts(k + 1):
                copy.start()

    whole = gram_cur[count] * (1.0 / cells)
    for j in range(DIRS):
        columns[j] = jnp.broadcast_to(whole[:, j:j + 1], (DIRS, 128))
    lane8 = lax.broadcasted_iota(jnp.int32, (8, 128), 1)
    cols = [jnp.broadcast_to(columns[k:DIRS, k:k + 1, :], (DIRS - k, 8, 128)) for k in range(DIRS)]
    rows = [
        jnp.broadcast_to(whole[i:i + 1], (8, 128)) + jnp.where(lane8 == 32 + i, 1.0, 0.0) for i in range(DIRS)
    ]
    for k in range(DIRS):
        scale = lax.rsqrt(cols[k][0])
        lower = cols[k] * scale[None]
        done = rows[k] * scale
        inverse_rows[k:k + 1, :] = done[0:1]
        for j in range(k + 1, DIRS):
            cols[j] = cols[j] - lower[j - k:] * lower[j - k][None]
            rows[j] = rows[j] - lower[j - k] * done
    solved = inverse_rows[...]
    for k in range(DIRS):
        spread[k] = jnp.broadcast_to(solved[:, 32 + k:33 + k], (DIRS, 128))

    collect(along_parts, along_cur, along_got, count - 1)
    along = along_cur[count] * (1.0 / cells)
    found = spread[0] * jnp.broadcast_to(along[0:1], (DIRS, 128))
    for k in range(1, DIRS):
        found = found + spread[k] * jnp.broadcast_to(along[k:k + 1], (DIRS, 128))
    for k in range(DIRS):
        weights[k] = jnp.broadcast_to(jnp.sum(spread[k] * found, axis=0, keepdims=True), (8, 128))

    def piece(t, _):
        for x in range(LAYERS):
            for h in range(2):
                p = BLOCKS * x + 2 * t + h
                value = w_all[DIRS, p]
                for k in range(DIRS):
                    value = value - weights[k] * w_all[k, p]
                shadow_ref[p] = value
                terms[t, 2 * x + h] = value + g_all[DIRS, p]
        return 0

    lax.fori_loop(0, segs, piece, 0)
    term_copies = [
        pltpu.make_async_remote_copy(
            terms.at[lax.rem(seg + d, segs)], arrived.at[d - 1], term_send.at[d - 1], term_recv.at[d - 1],
            device_id={"seg": lax.rem(seg + d, segs)}, device_id_type=MESH,
        )
        for d in range(1, segs)
    ]
    for copy in term_copies:
        copy.start()

    upper_ref[...] = jnp.where(lane >= lax.broadcasted_iota(jnp.int32, (DIRS, 128), 0), solved, 0.0)[:, 0:DIRS]
    diagonal = lane == lax.broadcasted_iota(jnp.int32, (DIRS, 128), 0)
    coef_ref[...] = jnp.sum(jnp.where(diagonal, found, 0.0), axis=0, keepdims=True)[:, 0:DIRS]

    for k in range(DIRS):
        for i in range(k, DIRS):
            inverse[i, k] = jnp.broadcast_to(spread[k, i:i + 1, :], (8, 128))

    def rows_at(q, _):
        spot = pl.ds(2 * q, 2)
        values = [w_all[k, spot] for k in range(DIRS)]
        for i in range(DIRS):
            total = inverse[i, 0][None] * values[0]
            for k in range(1, i + 1):
                total = total + inverse[i, k][None] * values[k]
            basis[i, spot] = total
        return 0

    stores = []
    for x in range(LAYERS):
        lax.fori_loop(x * BLOCKS // 2, (x + 1) * BLOCKS // 2, rows_at, 0)
        spot = pl.ds(BLOCKS * x, BLOCKS)
        store = pltpu.make_async_copy(basis.at[:, spot], basis_ref.at[:, spot], store_sem.at[x])
        store.start()
        stores.append(store)

    for copy in term_copies:
        copy.wait_recv()
    grad_ref[...] = terms[seg] + arrived[0] + arrived[1] + arrived[2]
    for copy in term_copies:
        copy.wait_send()
    for k in range(count):
        for copy in gram_parts(k) + along_parts(k):
            copy.wait_send()
    for store in stores:
        store.wait()


def body(directions, adjoint, velocity, diffusivity, objective_source, segment_start):
    size, segs = lax.axis_size("space"), lax.axis_size("seg")
    tile = (POS, 8, 128)
    cells = POS * 8 * 128 * size
    peers = sum(n - 1 for n in place_of(size))
    count = sum(n > 1 for n in place_of(size))
    hbm, vmem = pl.BlockSpec(memory_space=pl.ANY), pl.BlockSpec(memory_space=pltpu.VMEM)
    dma = pltpu.SemaphoreType.DMA
    outs = pl.pallas_call(
        functools.partial(kernel, size, segs, cells),
        out_shape=(
            jax.ShapeDtypeStruct((DIRS, *tile), F32),
            jax.ShapeDtypeStruct((DIRS, DIRS), F32),
            jax.ShapeDtypeStruct((1, DIRS), F32),
            jax.ShapeDtypeStruct(tile, F32),
            jax.ShapeDtypeStruct((2 * LAYERS, 8, 128), F32),
        ),
        in_specs=[pl.BlockSpec(memory_space=pltpu.SMEM)] + [hbm] * 5,
        out_specs=(hbm, vmem, vmem, vmem, vmem),
        scratch_shapes=[
            pltpu.VMEM((FIELDS, *tile), F32),
            pltpu.VMEM((FIELDS, *tile), F32),
            pltpu.VMEM((FIELDS, *tile), F32),
            pltpu.VMEM((2, FIELDS, BLOCKS, 8, 128), F32),
            pltpu.VMEM((2, FIELDS, BLOCKS, 8, 128), F32),
            pltpu.VMEM((2, 7, *tile), F32),
            pltpu.VMEM((3, *tile), F32),
            pltpu.VMEM(tile, F32),
            pltpu.VMEM(tile, F32),
            pltpu.VMEM((DIRS, *tile), F32),
            pltpu.VMEM((DIRS, 128), F32),
            pltpu.VMEM((count + 1, DIRS, 128), F32),
            pltpu.VMEM((peers, DIRS, 128), F32),
            pltpu.VMEM((count + 1, DIRS, 128), F32),
            pltpu.VMEM((peers, DIRS, 128), F32),
            pltpu.VMEM((DIRS, DIRS, 128), F32),
            pltpu.VMEM((DIRS, 128), F32),
            pltpu.VMEM((DIRS, DIRS, 128), F32),
            pltpu.VMEM((DIRS, DIRS, 8, 128), F32),
            pltpu.VMEM((DIRS, 8, 128), F32),
            pltpu.VMEM((4, 2 * LAYERS, 8, 128), F32),
            pltpu.VMEM((3, 2 * LAYERS, 8, 128), F32),
            dma((5,)), dma((LAYERS,)),
            dma((2, FIELDS)), dma((2, FIELDS)), dma((2, FIELDS)), dma((2, FIELDS)),
            dma((peers,)), dma((peers,)), dma((peers,)), dma((peers,)),
            dma((3,)), dma((3,)),
        ],
        compiler_params=pltpu.CompilerParams(
            collective_id=0, has_side_effects=True, vmem_limit_bytes=40 * 1024 * 1024
        ),
        cost_estimate=pl.CostEstimate(flops=120_000_000, bytes_accessed=5_200_000, transcendentals=64),
        name="shadowing",
    )(
        segment_start,
        directions.reshape(DIRS, *tile),
        adjoint.reshape(tile),
        velocity.reshape(3, *tile),
        diffusivity.reshape(tile),
        objective_source.reshape(tile),
    )
    basis_rows, upper, coefficients, shadow, gradient = outs
    return (
        basis_rows.reshape(directions.shape),
        upper[None],
        coefficients,
        shadow.reshape(adjoint.shape),
        gradient.reshape(LAYERS, 16, 128),
    )


def solution(mesh):
    return jax.shard_map(
        body,
        mesh=mesh,
        in_specs=(
            P("seg", None, "space", None, None),
            P("seg", "space", None, None),
            P("seg", None, "space", None, None),
            P("seg", "space", None, None),
            P("seg", "space", None, None),
            P("seg"),
        ),
        out_specs=(
            P("seg", None, "space", None, None),
            P("seg", None, None),
            P("seg", None),
            P("seg", "space", None, None),
            P("space", "seg", None),
        ),
        check_vma=False,
    )
```

time: 515 us -> 101 us (0.20)
  blocking collectives: 313 us -> 0 us
  waiting for transfers between devices: 121 us -> 0 us
  Pallas kernels: 0 us -> 90.4 us
  other arithmetic: 22.9 us -> 0 us
  between operations: 15.2 us -> 1.3 us
  starting transfers between devices: 13 us -> 0 us
  local copies, waits for them, and re-layouts: 20.1 us -> 8.99 us
  matrix products: 9.58 us -> 0 us
    psum x2 -> x0, blocking collectives: 313 us -> none  [the longest x1 159 us: body(): summed = lax.psum(partial_sums, 'space') / cell_count]
    pallas_call x0 -> x1, Pallas kernels: none -> 90.4 us  [body(): pl.pallas_call(functools.partial(kernel, size, segs, cells), out_shape=(j...]
    reduce_scatter x1 -> x0, waiting for transfers between devices: 85.9 us -> none  [body(): lax.psum_scatter(first_adjoint + shadow, 'seg', scatter_dimension=1, tile...]
    ppermute x4 -> x0, waiting for transfers between devices: 34.7 us -> none  [the longest x2 22.6 us: with_halo(): after = lax.ppermute(first, axis, down)]
    add x5 -> x0, other arithmetic: 13.3 us -> none  [the longest x2 11.4 us: advance(): return middle + diffusivity * laplace + 0.5 * strength * transport]
    ppermute x4 -> x0, starting transfers between devices: 12.9 us -> none  [the longest x2 12.9 us: with_halo(): after = lax.ppermute(first, axis, down)]
    dot_general x4 -> x0, matrix products: 9.38 us -> none  [the longest x1 2.87 us: body(): jnp.dot(flattened[:count_dirs], flattened[:count_dirs].T, precision=lax.P...]
    slice x10 -> x0, local copies, waits for them, and re-layouts: 6.21 us -> none  [the longest x2 2.01 us: advance(): forward_z = jnp.roll(middle, -1, axis=3)]
  transfers between devices with their start and end apart: 5 -> 0, of which waited for: 5 -> 0; matrix products, arithmetic and copies ran while one was open for 3% -> 0% of each run, Pallas kernels for 0% -> 0%
where the time goes in v1:
time: 101 us
  Pallas kernels  90.4 us (90%)
  local copies, waits for them, and re-layouts  8.99 us (9%)
  between operations  1.3 us (1%)
    pallas_call x1, Pallas kernels, body(): pl.pallas_call(functools.partial(kernel, size, segs, cells), out_shape=(j...  90.4 us
    unnamed x15, local copies, waits for them, and re-layouts  8.99 us

profile of v1, /device:TPU:1, one launch (start us, length us, event | category | flops | bytes accessed | tf_op | source)
XLA Modules:
  0.0 100.7 jit_solution(9291836293084004004)
XLA Ops:
  1.3 0.0 copy-start
  1.3 1.6 %copy-done = f32[1,16,4,64,128]{4,3,2,1,0:T(8,128)S(1)} copy-done((f32[1,16,4,64,128]{4,3,2,1,0:T(8,128)S(1)}, f32[1,16,4,64,128]{4,3,2,1,0:T(8,128)}, u32[]{:S(2)}) %copy-start) | copy-done | bytes 2097176
  2.9 0.0 copy-start.1
  2.9 1.0 copy-done.1
  3.9 0.0 copy-start.2
  3.9 0.9 copy-done.2
  4.8 0.0 copy-start.3
  4.8 0.9 copy-done.3
  5.7 0.0 copy-start.4
  5.7 0.9 copy-done.4
  6.6 90.4 %shadowing.1 = (f32[16,32,8,128]{3,2,1,0:T(8,128)S(1)}, f32[16,16]{1,0:T(8,128)S(1)}, f32[1,16]{1,0:T(1,128)S(1)}, f32[32,8,128]{2,1,0:T(8,128)S(1)}, f32[8,8,128]{2,1,0:T(8,128)S(1)}) custom-call(s32[1]{0:T(128)S(6)} %copy.16.start_ref, f32[16,32,8,128]{3,2,1,0:T(8,128)S(1)} %bitcast.9, f32[32,8,128]{2,1,0:T(8,128)S(1)} %bitcast.12, ...), custom_call_target="tpu_custom_call" | custom-call | flops 120000000 | bytes 5200000 | tf_op jit(solution)/shard_map/shadowing/pallas_call | solution.py:331
  97.0 1.3 %copy.17 = f32[1,16,4,64,128]{4,3,2,1,0:T(8,128)} copy(f32[1,16,4,64,128]{4,3,2,1,0:T(8,128)S(1)} %bitcast.10) | data formatting | bytes 4194304
  98.3 0.6 copy.18
  98.9 0.5 copy.19
  99.4 0.7 copy.20
  100.1 0.6 copy.21
Async XLA Ops:
  1.3 1.6 %copy-start = (f32[1,16,4,64,128]{4,3,2,1,0:T(8,128)S(1)}, f32[1,16,4,64,128]{4,3,2,1,0:T(8,128)}, u32[]{:S(2)}) copy-start(f32[1,16,4,64,128]{4,3,2,1,0:T(8,128)} %param.6) | copy-start | bytes 6291460
  2.9 1.0 copy-start.1
  3.9 0.9 copy-start.2
  4.8 0.9 copy-start.3
  5.7 0.9 copy-start.4

commit v2 on v1

--- a/solution.py
+++ b/solution.py
@@ -14,7 +14,6 @@
 LAYERS = 4
 BLOCKS = 8
 POS = LAYERS * BLOCKS
-AHEAD = 4
 F32 = jnp.float32
 
 
@@ -31,8 +30,10 @@
     x = lax.rem(lax.div(me, depth), width)
     y = lax.div(me, depth * width)
     stages = [
-        [(y * width + lax.rem(x + d, width)) * depth + z for d in range(1, width)],
-        [(lax.rem(y + d, height) * width + x) * depth + z for d in range(1, height)],
+        [
+            (lax.rem(y + a, height) * width + lax.rem(x + b, width)) * depth + z
+            for a in range(height) for b in range(width) if a or b
+        ],
         [(y * width + x) * depth + lax.rem(z + d, depth) for d in range(1, depth)],
     ]
     return [stage for stage in stages if stage]
@@ -53,9 +54,9 @@
     size, segs, cells,
     start_ref, dirs_ref, adj_ref, vel_ref, dif_ref, src_ref,
     basis_ref, upper_ref, coef_ref, shadow_ref, grad_ref,
-    f_all, g_all, w_all, f_halo, g_halo, coef, vel, dif, src, basis,
+    f_all, g_all, w_all, f_halo, g_halo, coef, vel, dif, src,
     gram, gram_cur, gram_got, along_cur, along_got, columns, inverse_rows, spread, inverse, weights, terms, arrived,
-    load_sem, store_sem, f_send, f_recv, g_send, g_recv,
+    load_sem, f_send, f_recv, g_send, g_recv,
     gram_send, gram_recv, along_send, along_recv, term_send, term_recv,
 ):
     seg = lax.axis_index("seg")
@@ -86,14 +87,11 @@
 
     lax.fori_loop(0, FIELDS, clear, 0)
     gram[...] = jnp.zeros_like(gram)
-    for load in loads:
-        load.wait()
     pl.semaphore_wait(barrier, len(greeted))
 
     def halo(source, landing, send, recv, n, side):
-        edge = BLOCKS * (LAYERS - 1) if side == 0 else 0
         return pltpu.make_async_remote_copy(
-            source.at[n, pl.ds(edge, BLOCKS)],
+            source,
             landing.at[side, n],
             send.at[side, n],
             recv.at[side, n],
@@ -101,12 +99,25 @@
             device_id_type=MESH,
         )
 
-    f_copy = functools.partial(halo, f_all, f_halo, f_send, f_recv)
-    g_copy = functools.partial(halo, g_all, g_halo, g_send, g_recv)
-    for n in range(AHEAD):
+    edges = (pl.ds(BLOCKS * (LAYERS - 1), BLOCKS), pl.ds(0, BLOCKS))
+
+    def f_copy(n, side):
+        source = adj_ref.at[edges[side]] if n is DIRS else dirs_ref.at[n, edges[side]]
+        return halo(source, f_halo, f_send, f_recv, n, side)
+
+    def g_copy(n, side):
+        return halo(g_all.at[n, edges[side]], g_halo, g_send, g_recv, n, side)
+
+    def begin(n, _):
         for side in range(2):
             f_copy(n, side).start()
-
+        return 0
+
+    lax.fori_loop(0, DIRS, begin, 0)
+    begin(DIRS, 0)
+
+    for load in loads:
+        load.wait()
     row = lax.broadcasted_iota(jnp.int32, (BLOCKS * 8, 128), 0)
     for step in range(2):
         phase = jnp.full((8, 128), start_ref[0], jnp.int32) + (1 - step)
@@ -135,58 +146,41 @@
             ahead = layer(source, (n,), x + 1) if x < LAYERS - 1 else landing[1, n].reshape(BLOCKS * 8, 128)
             behind = layer(source, (n,), x - 1) if x > 0 else landing[0, n].reshape(BLOCKS * 8, 128)
             out = stencil(here, ahead, behind, coef, step, x)
+            if n is DIRS:
+                out = out + layer(src, (), x)
             target[n, pl.ds(BLOCKS * x, BLOCKS)] = out.reshape(BLOCKS, 8, 128)
-
-        @pl.when(n == DIRS)
-        def _():
-            for x in layers:
-                spot = pl.ds(BLOCKS * x, BLOCKS)
-                target[n, spot] = target[n, spot] + src[spot]
 
     def first(n, _):
         for side in range(2):
             f_copy(n, side).wait_recv()
         advance(0, f_all, f_halo, g_all, n, (0, 3))
         for side in range(2):
-            f_copy(n, side).wait_send()
-
-        @pl.when(n + AHEAD < FIELDS)
-        def _():
-            for side in range(2):
-                f_copy(n + AHEAD, side).start()
-
-        @pl.when(n + AHEAD >= FIELDS)
-        def _():
-            for side in range(2):
-                g_copy(n + AHEAD - FIELDS, side).start()
-
+            g_copy(n, side).start()
         advance(0, f_all, f_halo, g_all, n, (1, 2))
         return 0
 
-    lax.fori_loop(0, FIELDS, first, 0)
+    lax.fori_loop(0, DIRS, first, 0)
+    first(DIRS, 0)
 
     lane = lax.broadcasted_iota(jnp.int32, (DIRS, 128), 1)
 
-    def products(n):
+    def products(n, low, total):
         def at(p, total):
             return total + w_all[0:DIRS, p] * w_all[n, p][None]
 
-        total = lax.fori_loop(0, POS, at, jnp.zeros((DIRS, 8, 128), F32), unroll=4)
-        return jnp.sum(jnp.sum(total, axis=1), axis=1, keepdims=True)
+        return lax.fori_loop(low, low + BLOCKS, at, total, unroll=4)
 
     def second(n):
         advance(1, g_all, g_halo, w_all, n, (1, 2))
+        total = jnp.zeros((DIRS, 8, 128), F32)
+        for x in (1, 2):
+            total = products(n, BLOCKS * x, total)
         for side in range(2):
             g_copy(n, side).wait_recv()
-            g_copy(n, side).wait_send()
-
-        @pl.when(n + AHEAD < FIELDS)
-        def _():
-            for side in range(2):
-                g_copy(n + AHEAD, side).start()
-
         advance(1, g_all, g_halo, w_all, n, (0, 3))
-        return products(n)
+        for x in (0, 3):
+            total = products(n, BLOCKS * x, total)
+        return jnp.sum(jnp.sum(total, axis=1), axis=1, keepdims=True)
 
     def gram_row(n, _):
         gram[...] = jnp.where(lane == n, second(n), gram[...])
@@ -297,16 +291,10 @@
             total = inverse[i, 0][None] * values[0]
             for k in range(1, i + 1):
                 total = total + inverse[i, k][None] * values[k]
-            basis[i, spot] = total
-        return 0
-
-    stores = []
-    for x in range(LAYERS):
-        lax.fori_loop(x * BLOCKS // 2, (x + 1) * BLOCKS // 2, rows_at, 0)
-        spot = pl.ds(BLOCKS * x, BLOCKS)
-        store = pltpu.make_async_copy(basis.at[:, spot], basis_ref.at[:, spot], store_sem.at[x])
-        store.start()
-        stores.append(store)
+            basis_ref[i, spot] = total
+        return 0
+
+    lax.fori_loop(0, POS // 2, rows_at, 0)
 
     for copy in term_copies:
         copy.wait_recv()
@@ -316,29 +304,55 @@
     for k in range(count):
         for copy in gram_parts(k) + along_parts(k):
             copy.wait_send()
-    for store in stores:
-        store.wait()
+
+    def sent(n, _):
+        for side in range(2):
+            f_copy(n, side).wait_send()
+            g_copy(n, side).wait_send()
+        return 0
+
+    lax.fori_loop(0, DIRS, sent, 0)
+    sent(DIRS, 0)
+
+
+def in_hbm(array):
+    return pltpu.with_memory_space_constraint(array, pltpu.HBM)
+
+
+def in_vmem(array):
+    return pltpu.with_memory_space_constraint(array, pltpu.VMEM)
+
+
+def store_kernel(*refs):
+    held, out, sems = refs[:5], refs[5:10], refs[10]
+    copies = [pltpu.make_async_copy(held[n], out[n], sems.at[n]) for n in range(5)]
+    for copy in copies:
+        copy.start()
+    for copy in copies:
+        copy.wait()
 
 
 def body(directions, adjoint, velocity, diffusivity, objective_source, segment_start):
     size, segs = lax.axis_size("space"), lax.axis_size("seg")
     tile = (POS, 8, 128)
     cells = POS * 8 * 128 * size
-    peers = sum(n - 1 for n in place_of(size))
-    count = sum(n > 1 for n in place_of(size))
-    hbm, vmem = pl.BlockSpec(memory_space=pl.ANY), pl.BlockSpec(memory_space=pltpu.VMEM)
+    height, width, depth = place_of(size)
+    groups = [n for n in (height * width, depth) if n > 1]
+    peers, count = sum(groups) - len(groups), len(groups)
+    hbm, vmem = pl.BlockSpec(memory_space=pltpu.HBM), pl.BlockSpec(memory_space=pltpu.VMEM)
     dma = pltpu.SemaphoreType.DMA
+    shapes = (
+        jax.ShapeDtypeStruct((DIRS, *tile), F32),
+        jax.ShapeDtypeStruct((DIRS, DIRS), F32),
+        jax.ShapeDtypeStruct((1, DIRS), F32),
+        jax.ShapeDtypeStruct(tile, F32),
+        jax.ShapeDtypeStruct((2 * LAYERS, 8, 128), F32),
+    )
     outs = pl.pallas_call(
         functools.partial(kernel, size, segs, cells),
-        out_shape=(
-            jax.ShapeDtypeStruct((DIRS, *tile), F32),
-            jax.ShapeDtypeStruct((DIRS, DIRS), F32),
-            jax.ShapeDtypeStruct((1, DIRS), F32),
-            jax.ShapeDtypeStruct(tile, F32),
-            jax.ShapeDtypeStruct((2 * LAYERS, 8, 128), F32),
-        ),
+        out_shape=tuple(pltpu.VMEM(s.shape, F32) for s in shapes),
         in_specs=[pl.BlockSpec(memory_space=pltpu.SMEM)] + [hbm] * 5,
-        out_specs=(hbm, vmem, vmem, vmem, vmem),
+        out_specs=(vmem,) * 5,
         scratch_shapes=[
             pltpu.VMEM((FIELDS, *tile), F32),
             pltpu.VMEM((FIELDS, *tile), F32),
@@ -349,7 +363,6 @@
             pltpu.VMEM((3, *tile), F32),
             pltpu.VMEM(tile, F32),
             pltpu.VMEM(tile, F32),
-            pltpu.VMEM((DIRS, *tile), F32),
             pltpu.VMEM((DIRS, 128), F32),
             pltpu.VMEM((count + 1, DIRS, 128), F32),
             pltpu.VMEM((peers, DIRS, 128), F32),
@@ -362,7 +375,7 @@
             pltpu.VMEM((DIRS, 8, 128), F32),
             pltpu.VMEM((4, 2 * LAYERS, 8, 128), F32),
             pltpu.VMEM((3, 2 * LAYERS, 8, 128), F32),
-            dma((5,)), dma((LAYERS,)),
+            dma((5,)),
             dma((2, FIELDS)), dma((2, FIELDS)), dma((2, FIELDS)), dma((2, FIELDS)),
             dma((peers,)), dma((peers,)), dma((peers,)), dma((peers,)),
             dma((3,)), dma((3,)),
@@ -374,13 +387,21 @@
         name="shadowing",
     )(
         segment_start,
-        directions.reshape(DIRS, *tile),
-        adjoint.reshape(tile),
-        velocity.reshape(3, *tile),
-        diffusivity.reshape(tile),
-        objective_source.reshape(tile),
+        in_hbm(directions.reshape(DIRS, *tile)),
+        in_hbm(adjoint.reshape(tile)),
+        in_hbm(velocity.reshape(3, *tile)),
+        in_hbm(diffusivity.reshape(tile)),
+        in_hbm(objective_source.reshape(tile)),
     )
-    basis_rows, upper, coefficients, shadow, gradient = outs
+    basis_rows, upper, coefficients, shadow, gradient = pl.pallas_call(
+        store_kernel,
+        out_shape=shapes,
+        in_specs=[pl.BlockSpec(memory_space=pl.ANY)] * 5,
+        out_specs=(hbm,) * 5,
+        scratch_shapes=[dma((5,))],
+        compiler_params=pltpu.CompilerParams(vmem_limit_bytes=1024 * 1024),
+        name="store",
+    )(*map(in_vmem, outs))
     return (
         basis_rows.reshape(directions.shape),
         upper[None],

time: 101 us -> 83.7 us (0.83)
  local copies, waits for them, and re-layouts: 8.99 us -> 0 us
  Pallas kernels: 90.4 us -> 82.4 us
    unnamed x15 -> x0, local copies, waits for them, and re-layouts: 8.99 us -> none
    pallas_call x1 -> x2, Pallas kernels: 90.4 us -> 82.4 us  [the longest x1 80.9 us: body(): pl.pallas_call(functools.partial(kernel, size, segs, cells), out_shape=tu...]
where the time goes in v2:
time: 83.7 us; the launch traced here: 83.6 us
  Pallas kernels  82.4 us (98%)
  between operations  1.29 us (2%)
    pallas_call x1, Pallas kernels, body(): pl.pallas_call(functools.partial(kernel, size, segs, cells), out_shape=tu...  80.9 us

profile of v2, /device:TPU:1, one launch (start us, length us, event | category | flops | bytes accessed | tf_op | source)
XLA Modules:
  0.0 83.6 jit_solution(10714074120291700751)
XLA Ops:
  1.3 80.9 %shadowing.1 = (f32[16,32,8,128]{3,2,1,0:T(8,128)S(1)}, f32[16,16]{1,0:T(8,128)S(1)}, f32[1,16]{1,0:T(1,128)S(1)}, f32[32,8,128]{2,1,0:T(8,128)S(1)}, f32[8,8,128]{2,1,0:T(8,128)S(1)}) custom-call(s32[1]{0:T(128)S(6)} %copy.11.start_ref, f32[16,32,8,128]{3,2,1,0:T(8,128)} %bitcast.9, f32[32,8,128]{2,1,0:T(8,128)} %bitcast.11, f32[3,32,8,128]{3,2,1,0:T(8,128)} %bitcast.10, ...), custom_call_target="tpu_custom_call" | custom-call | flops 120000000 | bytes 5200000 | tf_op jit(solution)/shard_map/shadowing/pallas_call | solution.py:351
  82.2 1.4 %store.1 = (f32[16,32,8,128]{3,2,1,0:T(8,128)}, f32[16,16]{1,0:T(8,128)}, f32[1,16]{1,0:T(1,128)}, f32[32,8,128]{2,1,0:T(8,128)}, f32[8,8,128]{2,1,0:T(8,128)}) custom-call(f32[16,32,8,128]{3,2,1,0:T(8,128)S(1)} %get-tuple-element.15.refs_0_, f32[16,16]{1,0:T(8,128)S(1)} %get-tuple-element.16.refs_1_, f32[1,16]{1,0:T(1,128)S(1)} %get-tuple-element.17.refs_2_, ...), custom_call_target="tpu_custom_call" | custom-call | tf_op jit(solution)/shard_map/store/pallas_call | solution.py:396

commit v3 on v2

--- a/solution.py
+++ b/solution.py
@@ -11,7 +11,10 @@
 MESH = pl.DeviceIdType.MESH
 DIRS = 16
 FIELDS = 17
+F_SIZE, G_SIZE = 4, 2
+F_GROUPS, G_GROUPS = DIRS // F_SIZE, DIRS // G_SIZE
 LAYERS = 4
+STORES = 1
 BLOCKS = 8
 POS = LAYERS * BLOCKS
 F32 = jnp.float32
@@ -92,7 +95,7 @@
     def halo(source, landing, send, recv, n, side):
         return pltpu.make_async_remote_copy(
             source,
-            landing.at[side, n],
+            landing,
             send.at[side, n],
             recv.at[side, n],
             device_id={"space": right if side == 0 else left},
@@ -102,19 +105,22 @@
     edges = (pl.ds(BLOCKS * (LAYERS - 1), BLOCKS), pl.ds(0, BLOCKS))
 
     def f_copy(n, side):
-        source = adj_ref.at[edges[side]] if n is DIRS else dirs_ref.at[n, edges[side]]
-        return halo(source, f_halo, f_send, f_recv, n, side)
+        if n is F_GROUPS:
+            return halo(adj_ref.at[edges[side]], f_halo.at[side, DIRS], f_send, f_recv, n, side)
+        fields = pl.ds(F_SIZE * n, F_SIZE)
+        return halo(dirs_ref.at[fields, edges[side]], f_halo.at[side, fields], f_send, f_recv, n, side)
 
     def g_copy(n, side):
-        return halo(g_all.at[n, edges[side]], g_halo, g_send, g_recv, n, side)
+        fields = DIRS if n is G_GROUPS else pl.ds(G_SIZE * n, G_SIZE)
+        return halo(g_all.at[fields, edges[side]], g_halo.at[side, fields], g_send, g_recv, n, side)
 
     def begin(n, _):
         for side in range(2):
             f_copy(n, side).start()
         return 0
 
-    lax.fori_loop(0, DIRS, begin, 0)
-    begin(DIRS, 0)
+    lax.fori_loop(0, F_GROUPS, begin, 0)
+    begin(F_GROUPS, 0)
 
     for load in loads:
         load.wait()
@@ -150,17 +156,28 @@
                 out = out + layer(src, (), x)
             target[n, pl.ds(BLOCKS * x, BLOCKS)] = out.reshape(BLOCKS, 8, 128)
 
-    def first(n, _):
-        for side in range(2):
-            f_copy(n, side).wait_recv()
-        advance(0, f_all, f_halo, g_all, n, (0, 3))
-        for side in range(2):
-            g_copy(n, side).start()
-        advance(0, f_all, f_halo, g_all, n, (1, 2))
-        return 0
-
-    lax.fori_loop(0, DIRS, first, 0)
-    first(DIRS, 0)
+    def first(group, fields):
+        for n in fields:
+            advance(0, f_all, f_halo, g_all, n, (0, 3))
+        for side in range(2):
+            g_copy(group, side).start()
+        for n in fields:
+            advance(0, f_all, f_halo, g_all, n, (1, 2))
+
+    def first_pair(p, _):
+        first(p, [G_SIZE * p + n for n in range(G_SIZE)])
+        return 0
+
+    def first_group(q, _):
+        for side in range(2):
+            f_copy(q, side).wait_recv()
+        ratio = F_SIZE // G_SIZE
+        return lax.fori_loop(ratio * q, ratio * (q + 1), first_pair, 0)
+
+    lax.fori_loop(0, F_GROUPS, first_group, 0)
+    for side in range(2):
+        f_copy(F_GROUPS, side).wait_recv()
+    first(G_GROUPS, [DIRS])
 
     lane = lax.broadcasted_iota(jnp.int32, (DIRS, 128), 1)
 
@@ -170,23 +187,33 @@
 
         return lax.fori_loop(low, low + BLOCKS, at, total, unroll=4)
 
-    def second(n):
-        advance(1, g_all, g_halo, w_all, n, (1, 2))
-        total = jnp.zeros((DIRS, 8, 128), F32)
-        for x in (1, 2):
-            total = products(n, BLOCKS * x, total)
-        for side in range(2):
-            g_copy(n, side).wait_recv()
-        advance(1, g_all, g_halo, w_all, n, (0, 3))
-        for x in (0, 3):
-            total = products(n, BLOCKS * x, total)
-        return jnp.sum(jnp.sum(total, axis=1), axis=1, keepdims=True)
-
-    def gram_row(n, _):
-        gram[...] = jnp.where(lane == n, second(n), gram[...])
-        return 0
-
-    lax.fori_loop(0, DIRS, gram_row, 0)
+    def second(group, fields):
+        totals = []
+        for n in fields:
+            advance(1, g_all, g_halo, w_all, n, (1, 2))
+            total = jnp.zeros((DIRS, 8, 128), F32)
+            if n is DIRS:
+                for x in (1, 2):
+                    total = products(n, BLOCKS * x, total)
+            totals.append(total)
+        for side in range(2):
+            g_copy(group, side).wait_recv()
+        for n in fields:
+            advance(1, g_all, g_halo, w_all, n, (0, 3))
+        sums = []
+        for n, total in zip(fields, totals):
+            for x in (0, 3) if n is DIRS else range(LAYERS):
+                total = products(n, BLOCKS * x, total)
+            sums.append(jnp.sum(jnp.sum(total, axis=1), axis=1, keepdims=True))
+        return sums
+
+    def gram_pair(p, _):
+        fields = [G_SIZE * p + n for n in range(G_SIZE)]
+        for n, column in zip(fields, second(p, fields)):
+            gram[...] = jnp.where(lane == n, column, gram[...])
+        return 0
+
+    lax.fori_loop(0, G_GROUPS, gram_pair, 0)
 
     def exchange(cur, got, send, recv, k):
         base = sum(len(stage) for stage in stages[:k])
@@ -210,10 +237,15 @@
             total = total + got[base + n]
         cur[k + 1] = total
 
-    gram_cur[0] = gram[...]
+    sublane = lax.broadcasted_iota(jnp.int32, (DIRS, 128), 0)
+    diagonal = lane == sublane
+    group_of = lane // DIRS == sublane % 8
+    packed = pltpu.roll(gram[...], 0, 1, stride=DIRS, stride_axis=0)
+    for h in range(2):
+        gram_cur[0, h:h + 1, :] = jnp.sum(packed[8 * h:8 * h + 8], axis=0, keepdims=True)
     for copy in gram_parts(0):
         copy.start()
-    along_cur[0] = jnp.broadcast_to(second(DIRS), (DIRS, 128))
+    along_cur[0] = jnp.sum(jnp.where(diagonal, second(G_GROUPS, [DIRS])[0], 0.0), axis=0, keepdims=True)
     for copy in along_parts(0):
         copy.start()
     count = len(stages)
@@ -226,7 +258,13 @@
             for copy in along_parts(k + 1):
                 copy.start()
 
-    whole = gram_cur[count] * (1.0 / cells)
+    packed = jnp.concatenate(
+        [jnp.broadcast_to(gram_cur[count, h:h + 1, :], (8, 128)) for h in range(2)], axis=0
+    )
+    whole = jnp.where(group_of, packed * (1.0 / cells), 0.0)
+    for bit in (1, 2, 4):
+        moved = pltpu.roll(whole, 128 - DIRS * bit, 1)
+        whole = jnp.where(lax.rem(sublane // bit, 2) == 1, moved, whole)
     for j in range(DIRS):
         columns[j] = jnp.broadcast_to(whole[:, j:j + 1], (DIRS, 128))
     lane8 = lax.broadcasted_iota(jnp.int32, (8, 128), 1)
@@ -248,13 +286,13 @@
 
     collect(along_parts, along_cur, along_got, count - 1)
     along = along_cur[count] * (1.0 / cells)
-    found = spread[0] * jnp.broadcast_to(along[0:1], (DIRS, 128))
-    for k in range(1, DIRS):
-        found = found + spread[k] * jnp.broadcast_to(along[k:k + 1], (DIRS, 128))
+    shifted = pltpu.roll(solved, 96, 1)
+    found = jnp.sum(shifted * along, axis=1, keepdims=True)
+    weight_row = jnp.sum(shifted * found, axis=0, keepdims=True)
     for k in range(DIRS):
-        weights[k] = jnp.broadcast_to(jnp.sum(spread[k] * found, axis=0, keepdims=True), (8, 128))
-
-    def piece(t, _):
+        weights[k] = jnp.broadcast_to(weight_row[:, k:k + 1], (8, 128))
+
+    def piece(t):
         for x in range(LAYERS):
             for h in range(2):
                 p = BLOCKS * x + 2 * t + h
@@ -263,9 +301,7 @@
                     value = value - weights[k] * w_all[k, p]
                 shadow_ref[p] = value
                 terms[t, 2 * x + h] = value + g_all[DIRS, p]
-        return 0
-
-    lax.fori_loop(0, segs, piece, 0)
+
     term_copies = [
         pltpu.make_async_remote_copy(
             terms.at[lax.rem(seg + d, segs)], arrived.at[d - 1], term_send.at[d - 1], term_recv.at[d - 1],
@@ -273,11 +309,12 @@
         )
         for d in range(1, segs)
     ]
-    for copy in term_copies:
-        copy.start()
-
-    upper_ref[...] = jnp.where(lane >= lax.broadcasted_iota(jnp.int32, (DIRS, 128), 0), solved, 0.0)[:, 0:DIRS]
-    diagonal = lane == lax.broadcasted_iota(jnp.int32, (DIRS, 128), 0)
+    for d in (2, 3, 1):
+        piece(lax.rem(seg + d, segs))
+        term_copies[d - 1].start()
+    piece(seg)
+
+    upper_ref[...] = jnp.where(lane >= sublane, solved, 0.0)[:, 0:DIRS]
     coef_ref[...] = jnp.sum(jnp.where(diagonal, found, 0.0), axis=0, keepdims=True)[:, 0:DIRS]
 
     for k in range(DIRS):
@@ -296,23 +333,28 @@
 
     lax.fori_loop(0, POS // 2, rows_at, 0)
 
+    def sent_f(n, _):
+        for side in range(2):
+            f_copy(n, side).wait_send()
+        return 0
+
+    def sent_g(n, _):
+        for side in range(2):
+            g_copy(n, side).wait_send()
+        return 0
+
+    lax.fori_loop(0, F_GROUPS, sent_f, 0)
+    sent_f(F_GROUPS, 0)
+    lax.fori_loop(0, G_GROUPS, sent_g, 0)
+    sent_g(G_GROUPS, 0)
+    for k in range(count):
+        for copy in gram_parts(k) + along_parts(k):
+            copy.wait_send()
     for copy in term_copies:
         copy.wait_recv()
     grad_ref[...] = terms[seg] + arrived[0] + arrived[1] + arrived[2]
     for copy in term_copies:
         copy.wait_send()
-    for k in range(count):
-        for copy in gram_parts(k) + along_parts(k):
-            copy.wait_send()
-
-    def sent(n, _):
-        for side in range(2):
-            f_copy(n, side).wait_send()
-            g_copy(n, side).wait_send()
-        return 0
-
-    lax.fori_loop(0, DIRS, sent, 0)
-    sent(DIRS, 0)
 
 
 def in_hbm(array):
@@ -325,7 +367,12 @@
 
 def store_kernel(*refs):
     held, out, sems = refs[:5], refs[5:10], refs[10]
-    copies = [pltpu.make_async_copy(held[n], out[n], sems.at[n]) for n in range(5)]
+    part = DIRS // STORES
+    copies = [
+        pltpu.make_async_copy(held[0].at[pl.ds(part * n, part)], out[0].at[pl.ds(part * n, part)], sems.at[n])
+        for n in range(STORES)
+    ]
+    copies += [pltpu.make_async_copy(held[n], out[n], sems.at[STORES + n - 1]) for n in range(1, 5)]
     for copy in copies:
         copy.start()
     for copy in copies:
@@ -364,10 +411,10 @@
             pltpu.VMEM(tile, F32),
             pltpu.VMEM(tile, F32),
             pltpu.VMEM((DIRS, 128), F32),
-            pltpu.VMEM((count + 1, DIRS, 128), F32),
-            pltpu.VMEM((peers, DIRS, 128), F32),
-            pltpu.VMEM((count + 1, DIRS, 128), F32),
-            pltpu.VMEM((peers, DIRS, 128), F32),
+            pltpu.VMEM((count + 1, 2, 128), F32),
+            pltpu.VMEM((peers, 2, 128), F32),
+            pltpu.VMEM((count + 1, 1, 128), F32),
+            pltpu.VMEM((peers, 1, 128), F32),
             pltpu.VMEM((DIRS, DIRS, 128), F32),
             pltpu.VMEM((DIRS, 128), F32),
             pltpu.VMEM((DIRS, DIRS, 128), F32),
@@ -376,7 +423,7 @@
             pltpu.VMEM((4, 2 * LAYERS, 8, 128), F32),
             pltpu.VMEM((3, 2 * LAYERS, 8, 128), F32),
             dma((5,)),
-            dma((2, FIELDS)), dma((2, FIELDS)), dma((2, FIELDS)), dma((2, FIELDS)),
+            dma((2, F_GROUPS + 1)), dma((2, F_GROUPS + 1)), dma((2, G_GROUPS + 1)), dma((2, G_GROUPS + 1)),
             dma((peers,)), dma((peers,)), dma((peers,)), dma((peers,)),
             dma((3,)), dma((3,)),
         ],
@@ -398,7 +445,7 @@
         out_shape=shapes,
         in_specs=[pl.BlockSpec(memory_space=pl.ANY)] * 5,
         out_specs=(hbm,) * 5,
-        scratch_shapes=[dma((5,))],
+        scratch_shapes=[dma((STORES + 4,))],
         compiler_params=pltpu.CompilerParams(vmem_limit_bytes=1024 * 1024),
         name="store",
     )(*map(in_vmem, outs))

time: 83.7 us -> 82.4 us (0.984)
  Pallas kernels: 82.4 us -> 81 us
    pallas_call x1, Pallas kernels: 80.9 us -> 79.6 us  [body(): pl.pallas_call(functools.partial(kernel, size, segs, cells), out_shape=tu...]
where the time goes in v3:
time: 82.4 us; the launch traced here: 82.3 us
  Pallas kernels  81 us (98%)
  between operations  1.29 us (2%)
    pallas_call x1, Pallas kernels, body(): pl.pallas_call(functools.partial(kernel, size, segs, cells), out_shape=tu...  79.6 us

profile of v3, /device:TPU:1, one launch (start us, length us, event | category | flops | bytes accessed | tf_op | source)
XLA Modules:
  0.0 82.3 jit_solution(2964392188741447393)
XLA Ops:
  1.3 79.6 %shadowing.1 = (f32[16,32,8,128]{3,2,1,0:T(8,128)S(1)}, f32[16,16]{1,0:T(8,128)S(1)}, f32[1,16]{1,0:T(1,128)S(1)}, f32[32,8,128]{2,1,0:T(8,128)S(1)}, f32[8,8,128]{2,1,0:T(8,128)S(1)}) custom-call(s32[1]{0:T(128)S(6)} %copy.11.start_ref, f32[16,32,8,128]{3,2,1,0:T(8,128)} %bitcast.9, f32[32,8,128]{2,1,0:T(8,128)} %bitcast.11, f32[3,32,8,128]{3,2,1,0:T(8,128)} %bitcast.10, ...), custom_call_target="tpu_custom_call" | custom-call | flops 120000000 | bytes 5200000 | tf_op jit(solution)/shard_map/shadowing/pallas_call | solution.py:398
  80.9 1.4 %store.1 = (f32[16,32,8,128]{3,2,1,0:T(8,128)}, f32[16,16]{1,0:T(8,128)}, f32[1,16]{1,0:T(1,128)}, f32[32,8,128]{2,1,0:T(8,128)}, f32[8,8,128]{2,1,0:T(8,128)}) custom-call(f32[16,32,8,128]{3,2,1,0:T(8,128)S(1)} %get-tuple-element.15.refs_0_, f32[16,16]{1,0:T(8,128)S(1)} %get-tuple-element.16.refs_1_, f32[1,16]{1,0:T(1,128)S(1)} %get-tuple-element.17.refs_2_, ...), custom_call_target="tpu_custom_call" | custom-call | tf_op jit(solution)/shard_map/store/pallas_call | solution.py:443

commit v4 on v3

--- a/solution.py
+++ b/solution.py
@@ -34,10 +34,13 @@
     y = lax.div(me, depth * width)
     stages = [
         [
-            (lax.rem(y + a, height) * width + lax.rem(x + b, width)) * depth + z
-            for a in range(height) for b in range(width) if a or b
+            ((y + 1 - 2 * lax.rem(y, 2) if a else y) * width + lax.rem(x + b, width)) * depth + z
+            for a in range(2) for b in range(width) if a or b
         ],
-        [(y * width + x) * depth + lax.rem(z + d, depth) for d in range(1, depth)],
+        [
+            ((height - 1 - y if a else y) * width + x) * depth + lax.rem(z + d, depth)
+            for a in range(2) for d in range(depth) if a or d
+        ],
     ]
     return [stage for stage in stages if stage]
 
@@ -67,6 +70,14 @@
     right, left = lax.rem(me + 1, size), lax.rem(me + size - 1, size)
     stages = peers_of(me, size)
 
+    barrier = pltpu.get_barrier_semaphore()
+    greeted = [{"space": left}, {"space": right}]
+    greeted += [{"space": peer} for stage in stages for peer in stage]
+    partners = [lax.rem(seg + 2, segs), segs - 1 - seg, seg + 1 - 2 * lax.rem(seg, 2)]
+    greeted += [{"seg": partner} for partner in partners]
+    for device in greeted:
+        pl.semaphore_signal(barrier, inc=1, device_id=device, device_id_type=MESH)
+
     loads = [
         pltpu.make_async_copy(dirs_ref, f_all.at[pl.ds(0, DIRS)], load_sem.at[0]),
         pltpu.make_async_copy(adj_ref, f_all.at[DIRS], load_sem.at[1]),
@@ -76,13 +87,6 @@
     ]
     for load in loads:
         load.start()
-
-    barrier = pltpu.get_barrier_semaphore()
-    greeted = [{"space": left}, {"space": right}]
-    greeted += [{"space": peer} for stage in stages for peer in stage]
-    greeted += [{"seg": lax.rem(seg + d, segs)} for d in range(1, segs)]
-    for device in greeted:
-        pl.semaphore_signal(barrier, inc=1, device_id=device, device_id_type=MESH)
 
     def clear(n, _):
         w_all[n] = jnp.zeros((POS, 8, 128), F32)
@@ -152,68 +156,48 @@
             ahead = layer(source, (n,), x + 1) if x < LAYERS - 1 else landing[1, n].reshape(BLOCKS * 8, 128)
             behind = layer(source, (n,), x - 1) if x > 0 else landing[0, n].reshape(BLOCKS * 8, 128)
             out = stencil(here, ahead, behind, coef, step, x)
-            if n is DIRS:
-                out = out + layer(src, (), x)
             target[n, pl.ds(BLOCKS * x, BLOCKS)] = out.reshape(BLOCKS, 8, 128)
 
-    def first(group, fields):
-        for n in fields:
-            advance(0, f_all, f_halo, g_all, n, (0, 3))
+        @pl.when(n == DIRS)
+        def _():
+            for x in layers:
+                spot = pl.ds(BLOCKS * x, BLOCKS)
+                target[n, spot] = target[n, spot] + src[spot]
+
+    def each(p, work):
+        def one(n, _):
+            work(n)
+            return 0
+
+        lax.fori_loop(G_SIZE * p, jnp.minimum(G_SIZE * (p + 1), FIELDS), one, 0)
+
+    def either(p, work):
+        pl.when(p < G_GROUPS)(lambda: work(p))
+        pl.when(p == G_GROUPS)(lambda: work(G_GROUPS))
+
+    def both_sides(action):
         for side in range(2):
-            g_copy(group, side).start()
-        for n in fields:
-            advance(0, f_all, f_halo, g_all, n, (1, 2))
-
-    def first_pair(p, _):
-        first(p, [G_SIZE * p + n for n in range(G_SIZE)])
-        return 0
-
-    def first_group(q, _):
-        for side in range(2):
-            f_copy(q, side).wait_recv()
-        ratio = F_SIZE // G_SIZE
-        return lax.fori_loop(ratio * q, ratio * (q + 1), first_pair, 0)
-
-    lax.fori_loop(0, F_GROUPS, first_group, 0)
-    for side in range(2):
-        f_copy(F_GROUPS, side).wait_recv()
-    first(G_GROUPS, [DIRS])
+            action(side)
+
+    ratio = F_SIZE // G_SIZE
+
+    def first(p, _):
+        @pl.when(jnp.logical_and(p < G_GROUPS, lax.rem(p, ratio) == 0))
+        def _():
+            both_sides(lambda side: f_copy(lax.div(p, ratio), side).wait_recv())
+
+        @pl.when(p == G_GROUPS)
+        def _():
+            both_sides(lambda side: f_copy(F_GROUPS, side).wait_recv())
+
+        each(p, lambda n: advance(0, f_all, f_halo, g_all, n, (0, 3)))
+        either(p, lambda group: both_sides(lambda side: g_copy(group, side).start()))
+        each(p, lambda n: advance(0, f_all, f_halo, g_all, n, (1, 2)))
+        return 0
+
+    lax.fori_loop(0, G_GROUPS + 1, first, 0)
 
     lane = lax.broadcasted_iota(jnp.int32, (DIRS, 128), 1)
-
-    def products(n, low, total):
-        def at(p, total):
-            return total + w_all[0:DIRS, p] * w_all[n, p][None]
-
-        return lax.fori_loop(low, low + BLOCKS, at, total, unroll=4)
-
-    def second(group, fields):
-        totals = []
-        for n in fields:
-            advance(1, g_all, g_halo, w_all, n, (1, 2))
-            total = jnp.zeros((DIRS, 8, 128), F32)
-            if n is DIRS:
-                for x in (1, 2):
-                    total = products(n, BLOCKS * x, total)
-            totals.append(total)
-        for side in range(2):
-            g_copy(group, side).wait_recv()
-        for n in fields:
-            advance(1, g_all, g_halo, w_all, n, (0, 3))
-        sums = []
-        for n, total in zip(fields, totals):
-            for x in (0, 3) if n is DIRS else range(LAYERS):
-                total = products(n, BLOCKS * x, total)
-            sums.append(jnp.sum(jnp.sum(total, axis=1), axis=1, keepdims=True))
-        return sums
-
-    def gram_pair(p, _):
-        fields = [G_SIZE * p + n for n in range(G_SIZE)]
-        for n, column in zip(fields, second(p, fields)):
-            gram[...] = jnp.where(lane == n, column, gram[...])
-        return 0
-
-    lax.fori_loop(0, G_GROUPS, gram_pair, 0)
 
     def exchange(cur, got, send, recv, k):
         base = sum(len(stage) for stage in stages[:k])
@@ -240,12 +224,32 @@
     sublane = lax.broadcasted_iota(jnp.int32, (DIRS, 128), 0)
     diagonal = lane == sublane
     group_of = lane // DIRS == sublane % 8
-    packed = pltpu.roll(gram[...], 0, 1, stride=DIRS, stride_axis=0)
-    for h in range(2):
-        gram_cur[0, h:h + 1, :] = jnp.sum(packed[8 * h:8 * h + 8], axis=0, keepdims=True)
-    for copy in gram_parts(0):
-        copy.start()
-    along_cur[0] = jnp.sum(jnp.where(diagonal, second(G_GROUPS, [DIRS])[0], 0.0), axis=0, keepdims=True)
+    def gram_row(n):
+        def at(p, total):
+            return total + w_all[0:DIRS, p] * w_all[n, p][None]
+
+        total = lax.fori_loop(0, POS, at, jnp.zeros((DIRS, 8, 128), F32), unroll=4)
+        column = jnp.sum(jnp.sum(total, axis=1), axis=1, keepdims=True)
+        gram[...] = jnp.where(lane == n, column, gram[...])
+
+    def second(p, _):
+        @pl.when(p == G_GROUPS)
+        def _():
+            packed = pltpu.roll(gram[...], 0, 1, stride=DIRS, stride_axis=0)
+            for h in range(2):
+                gram_cur[0, h:h + 1, :] = jnp.sum(packed[8 * h:8 * h + 8], axis=0, keepdims=True)
+            for copy in gram_parts(0):
+                copy.start()
+
+        each(p, lambda n: advance(1, g_all, g_halo, w_all, n, (1, 2)))
+        either(p, lambda group: both_sides(lambda side: g_copy(group, side).wait_recv()))
+        each(p, lambda n: advance(1, g_all, g_halo, w_all, n, (0, 3)))
+        each(p, gram_row)
+        return 0
+
+    lax.fori_loop(0, G_GROUPS + 1, second, 0)
+    along_column = jnp.broadcast_to(gram[:, DIRS:DIRS + 1], (DIRS, 128))
+    along_cur[0] = jnp.sum(jnp.where(diagonal, along_column, 0.0), axis=0, keepdims=True)
     for copy in along_parts(0):
         copy.start()
     count = len(stages)
@@ -304,14 +308,14 @@
 
     term_copies = [
         pltpu.make_async_remote_copy(
-            terms.at[lax.rem(seg + d, segs)], arrived.at[d - 1], term_send.at[d - 1], term_recv.at[d - 1],
-            device_id={"seg": lax.rem(seg + d, segs)}, device_id_type=MESH,
+            terms.at[partner], arrived.at[n], term_send.at[n], term_recv.at[n],
+            device_id={"seg": partner}, device_id_type=MESH,
         )
-        for d in range(1, segs)
+        for n, partner in enumerate(partners)
     ]
-    for d in (2, 3, 1):
-        piece(lax.rem(seg + d, segs))
-        term_copies[d - 1].start()
+    for partner, copy in zip(partners, term_copies):
+        piece(partner)
+        copy.start()
     piece(seg)
 
     upper_ref[...] = jnp.where(lane >= sublane, solved, 0.0)[:, 0:DIRS]
@@ -384,7 +388,7 @@
     tile = (POS, 8, 128)
     cells = POS * 8 * 128 * size
     height, width, depth = place_of(size)
-    groups = [n for n in (height * width, depth) if n > 1]
+    groups = [8, 8]
     peers, count = sum(groups) - len(groups), len(groups)
     hbm, vmem = pl.BlockSpec(memory_space=pltpu.HBM), pl.BlockSpec(memory_space=pltpu.VMEM)
     dma = pltpu.SemaphoreType.DMA

time: 82.4 us -> 82.3 us (level)
  no operation moved by 1% of the time
where the time goes in v4:
time: 82.3 us; the launch traced here: 82.2 us
  Pallas kernels  80.9 us (98%)
  between operations  1.29 us (2%)
    pallas_call x1, Pallas kernels, body(): pl.pallas_call(functools.partial(kernel, size, segs, cells), out_shape=tu...  79.5 us

profile of v4, /device:TPU:1, one launch (start us, length us, event | category | flops | bytes accessed | tf_op | source)
XLA Modules:
  0.0 82.2 jit_solution(15167671668938754350)
XLA Ops:
  1.3 79.5 %shadowing.1 = (f32[16,32,8,128]{3,2,1,0:T(8,128)S(1)}, f32[16,16]{1,0:T(8,128)S(1)}, f32[1,16]{1,0:T(1,128)S(1)}, f32[32,8,128]{2,1,0:T(8,128)S(1)}, f32[8,8,128]{2,1,0:T(8,128)S(1)}) custom-call(s32[1]{0:T(128)S(6)} %copy.11.start_ref, f32[16,32,8,128]{3,2,1,0:T(8,128)} %bitcast.9, f32[32,8,128]{2,1,0:T(8,128)} %bitcast.11, f32[3,32,8,128]{3,2,1,0:T(8,128)} %bitcast.10, ...), custom_call_target="tpu_custom_call" | custom-call | flops 120000000 | bytes 5200000 | tf_op jit(solution)/shard_map/shadowing/pallas_call | solution.py:402
  80.8 1.4 %store.1 = (f32[16,32,8,128]{3,2,1,0:T(8,128)}, f32[16,16]{1,0:T(8,128)}, f32[1,16]{1,0:T(1,128)}, f32[32,8,128]{2,1,0:T(8,128)}, f32[8,8,128]{2,1,0:T(8,128)}) custom-call(f32[16,32,8,128]{3,2,1,0:T(8,128)S(1)} %get-tuple-element.15.refs_0_, f32[16,16]{1,0:T(8,128)S(1)} %get-tuple-element.16.refs_1_, f32[1,16]{1,0:T(1,128)S(1)} %get-tuple-element.17.refs_2_, ...), custom_call_target="tpu_custom_call" | custom-call | tf_op jit(solution)/shard_map/store/pallas_call | solution.py:447

commit v5 on v4

--- a/solution.py
+++ b/solution.py
@@ -94,6 +94,8 @@
 
     lax.fori_loop(0, FIELDS, clear, 0)
     gram[...] = jnp.zeros_like(gram)
+    for load in loads:
+        load.wait()
     pl.semaphore_wait(barrier, len(greeted))
 
     def halo(source, landing, send, recv, n, side):
@@ -110,9 +112,9 @@
 
     def f_copy(n, side):
         if n is F_GROUPS:
-            return halo(adj_ref.at[edges[side]], f_halo.at[side, DIRS], f_send, f_recv, n, side)
+            return halo(f_all.at[DIRS, edges[side]], f_halo.at[side, DIRS], f_send, f_recv, n, side)
         fields = pl.ds(F_SIZE * n, F_SIZE)
-        return halo(dirs_ref.at[fields, edges[side]], f_halo.at[side, fields], f_send, f_recv, n, side)
+        return halo(f_all.at[fields, edges[side]], f_halo.at[side, fields], f_send, f_recv, n, side)
 
     def g_copy(n, side):
         fields = DIRS if n is G_GROUPS else pl.ds(G_SIZE * n, G_SIZE)
@@ -126,8 +128,6 @@
     lax.fori_loop(0, F_GROUPS, begin, 0)
     begin(F_GROUPS, 0)
 
-    for load in loads:
-        load.wait()
     row = lax.broadcasted_iota(jnp.int32, (BLOCKS * 8, 128), 0)
     for step in range(2):
         phase = jnp.full((8, 128), start_ref[0], jnp.int32) + (1 - step)

time: 82.3 us -> 82.1 us (level)
  no operation moved by 1% of the time
where the time goes in v5:
time: 82.1 us; the launch traced here: 82 us
  Pallas kernels  80.7 us (98%)
  between operations  1.29 us (2%)
    pallas_call x1, Pallas kernels, body(): pl.pallas_call(functools.partial(kernel, size, segs, cells), out_shape=tu...  79.3 us

profile of v5, /device:TPU:1, one launch (start us, length us, event | category | flops | bytes accessed | tf_op | source)
XLA Modules:
  0.0 82.0 jit_solution(16919992961280427436)
XLA Ops:
  1.3 79.3 %shadowing.1 = (f32[16,32,8,128]{3,2,1,0:T(8,128)S(1)}, f32[16,16]{1,0:T(8,128)S(1)}, f32[1,16]{1,0:T(1,128)S(1)}, f32[32,8,128]{2,1,0:T(8,128)S(1)}, f32[8,8,128]{2,1,0:T(8,128)S(1)}) custom-call(s32[1]{0:T(128)S(6)} %copy.11.start_ref, f32[16,32,8,128]{3,2,1,0:T(8,128)} %bitcast.9, f32[32,8,128]{2,1,0:T(8,128)} %bitcast.11, f32[3,32,8,128]{3,2,1,0:T(8,128)} %bitcast.10, ...), custom_call_target="tpu_custom_call" | custom-call | flops 120000000 | bytes 5200000 | tf_op jit(solution)/shard_map/shadowing/pallas_call | solution.py:402
  80.6 1.4 %store.1 = (f32[16,32,8,128]{3,2,1,0:T(8,128)}, f32[16,16]{1,0:T(8,128)}, f32[1,16]{1,0:T(1,128)}, f32[32,8,128]{2,1,0:T(8,128)}, f32[8,8,128]{2,1,0:T(8,128)}) custom-call(f32[16,32,8,128]{3,2,1,0:T(8,128)S(1)} %get-tuple-element.15.refs_0_, f32[16,16]{1,0:T(8,128)S(1)} %get-tuple-element.16.refs_1_, f32[1,16]{1,0:T(1,128)S(1)} %get-tuple-element.17.refs_2_, ...), custom_call_target="tpu_custom_call" | custom-call | tf_op jit(solution)/shard_map/store/pallas_call | solution.py:447

commit v6 on v5

--- a/solution.py
+++ b/solution.py
@@ -35,11 +35,11 @@
     stages = [
         [
             ((y + 1 - 2 * lax.rem(y, 2) if a else y) * width + lax.rem(x + b, width)) * depth + z
-            for a in range(2) for b in range(width) if a or b
+            for a, b in ((1, 2), (1, 1), (1, 3), (0, 2), (1, 0), (0, 1), (0, 3))
         ],
         [
             ((height - 1 - y if a else y) * width + x) * depth + lax.rem(z + d, depth)
-            for a in range(2) for d in range(depth) if a or d
+            for a, d in ((1, 1), (1, 3), (1, 2), (0, 1), (0, 3), (0, 2), (1, 0))
         ],
     ]
     return [stage for stage in stages if stage]
@@ -72,9 +72,9 @@
 
     barrier = pltpu.get_barrier_semaphore()
     greeted = [{"space": left}, {"space": right}]
-    greeted += [{"space": peer} for stage in stages for peer in stage]
     partners = [lax.rem(seg + 2, segs), segs - 1 - seg, seg + 1 - 2 * lax.rem(seg, 2)]
     greeted += [{"seg": partner} for partner in partners]
+    greeted += [{"space": peer} for stage in reversed(stages) for peer in stage]
     for device in greeted:
         pl.semaphore_signal(barrier, inc=1, device_id=device, device_id_type=MESH)
 

time: 82.1 us -> 82 us (level)
  no operation moved by 1% of the time
where the time goes in v6:
time: 82 us; the launch traced here: 81.9 us
  Pallas kernels  80.6 us (98%)
  between operations  1.29 us (2%)
    pallas_call x1, Pallas kernels, body(): pl.pallas_call(functools.partial(kernel, size, segs, cells), out_shape=tu...  79.2 us

profile of v6, /device:TPU:1, one launch (start us, length us, event | category | flops | bytes accessed | tf_op | source)
XLA Modules:
  0.0 81.9 jit_solution(11207221241966315971)
XLA Ops:
  1.3 79.2 %shadowing.1 = (f32[16,32,8,128]{3,2,1,0:T(8,128)S(1)}, f32[16,16]{1,0:T(8,128)S(1)}, f32[1,16]{1,0:T(1,128)S(1)}, f32[32,8,128]{2,1,0:T(8,128)S(1)}, f32[8,8,128]{2,1,0:T(8,128)S(1)}) custom-call(s32[1]{0:T(128)S(6)} %copy.11.start_ref, f32[16,32,8,128]{3,2,1,0:T(8,128)} %bitcast.9, f32[32,8,128]{2,1,0:T(8,128)} %bitcast.11, f32[3,32,8,128]{3,2,1,0:T(8,128)} %bitcast.10, ...), custom_call_target="tpu_custom_call" | custom-call | flops 120000000 | bytes 5200000 | tf_op jit(solution)/shard_map/shadowing/pallas_call | solution.py:402
  80.5 1.4 %store.1 = (f32[16,32,8,128]{3,2,1,0:T(8,128)}, f32[16,16]{1,0:T(8,128)}, f32[1,16]{1,0:T(1,128)}, f32[32,8,128]{2,1,0:T(8,128)}, f32[8,8,128]{2,1,0:T(8,128)}) custom-call(f32[16,32,8,128]{3,2,1,0:T(8,128)S(1)} %get-tuple-element.15.refs_0_, f32[16,16]{1,0:T(8,128)S(1)} %get-tuple-element.16.refs_1_, f32[1,16]{1,0:T(1,128)S(1)} %get-tuple-element.17.refs_2_, ...), custom_call_target="tpu_custom_call" | custom-call | tf_op jit(solution)/shard_map/store/pallas_call | solution.py:447
